TPU v7x, 256 devices: a whole 4x4x8 slice. The times are simulated.
256 devices in a mesh: ctx: 64 (over x, z, core), dp: 4 (over y).
Axes of the slice: x: 4, y: 4, z: 8, core: 2. Of those that a mesh axis runs over, the one named last changes fastest.
Arguments:
- projected: bfloat16 [65536, 12288], P(('dp', 'ctx')), parts along dimension 0, may hold values from -6 to 6
- taps: float32 [7, 12288], replicated, may hold values from -2 to 2
- decays: float32 [4096, 16], replicated, may hold values from 3.0517578e-05 to 0.033
- residues: float32 [4096, 16], replicated, may hold values from -1.5 to 1.5
Outputs:
- mixed: float32 [65536, 4096], P(('dp', 'ctx')), parts along dimension 0
There are 4 independent parts, one for each index of `dp`. A program takes and returns all parts, laid end to end along the dimension named above; an argument that names none is the same for every part. Nothing has to cross between parts.
All inputs are finite; a program needn't handle non-finite values.
Results may differ from a plain program's by a relative error of at most 0.0041.
Values may be sent and summed in bfloat16 or wider, within the bound.
A program may use at most 128 MiB of HBM per device.

v0:
```python
import jax
import jax.numpy as jnp
import ml_dtypes
import numpy as np
from jax import lax
from jax.sharding import PartitionSpec as P

NODES = 13


def chunk_basis(length):
    place = np.cos((np.arange(NODES) + 0.5) * np.pi / NODES)
    nodes = 0.5 * (length - 1) * (1.0 + place)
    token = np.arange(length)
    basis = np.ones((length, NODES))
    for j in range(NODES):
        for k in range(NODES):
            if k != j:
                basis[:, j] *= (token - nodes[k]) / (nodes[j] - nodes[k])
    return nodes, basis


def split_pair(table):
    high = table.astype(ml_dtypes.bfloat16)
    low = (table - high.astype(np.float64)).astype(ml_dtypes.bfloat16)
    return high, low


def short_filter(projected, taps):
    lead = taps.shape[0] - 1
    rows = projected.shape[0]
    peers = lax.axis_size("ctx")
    edge = lax.ppermute(projected[rows - lead :], "ctx", [(i, i + 1) for i in range(peers - 1)])
    joined = jnp.concatenate([edge, projected], 0)
    total = jnp.zeros(projected.shape, jnp.float32)
    for shift in range(taps.shape[0]):
        total = total + taps[shift][None, :] * joined[lead - shift : lead - shift + rows].astype(jnp.float32)
    return total


def mm(a, b):
    return jnp.dot(a, b, preferred_element_type=jnp.float32)


def shards(projected, taps, decays, residues):
    rows = projected.shape[0]
    width = taps.shape[1] // 3
    peers = lax.axis_size("ctx")
    own = width // peers
    nodes, basis = chunk_basis(rows)
    lag = np.arange(rows)[:, None] - np.arange(rows)[None, :]
    toeplitz = np.where(lag[None] >= 0, basis.T[:, np.maximum(lag, 0)], 0.0)
    node = jnp.asarray(nodes, jnp.float32)

    filtered = short_filter(projected, taps)
    queries = filtered[:, :width]
    gated = (filtered[:, width : 2 * width] * filtered[:, 2 * width :]).astype(jnp.bfloat16)

    high, low = split_pair(basis)
    moments = mm(jnp.asarray(high.T), gated) + mm(jnp.asarray(low.T), gated)
    moved = lax.all_to_all(moments, "ctx", split_axis=1, concat_axis=0, tiled=True)
    moved = moved.reshape(peers, NODES, own)

    start = lax.axis_index("ctx") * own
    rates = lax.dynamic_slice_in_dim(decays, start, own, 0)
    weights = lax.dynamic_slice_in_dim(residues, start, own, 0)
    weights = weights * jnp.sqrt(-jnp.expm1(-2.0 * rates))
    into = jnp.exp(-rates[:, :, None] * (rows - 1 - node))
    states = jnp.einsum("djc,crj->dcr", moved, into, precision=lax.Precision.HIGHEST)
    step = jnp.exp(-rates * rows)

    def advance(state, fresh):
        return step * state + fresh, state

    _, held = lax.scan(advance, jnp.zeros_like(states[0]), states)
    out_of = weights[:, :, None] * jnp.exp(-rates[:, :, None] * (1.0 + node))
    past = jnp.einsum("dcr,crj->djc", held, out_of, precision=lax.Precision.HIGHEST)
    past = past.reshape(peers * NODES, own)
    past = lax.all_to_all(past, "ctx", split_axis=0, concat_axis=1, tiled=True)

    all_weights = residues * jnp.sqrt(-jnp.expm1(-2.0 * decays))
    coef = jnp.sum(all_weights[None] * jnp.exp(-decays[None] * node[:, None, None]), 2)
    result = jnp.dot(jnp.asarray(basis, jnp.float32), past, precision=lax.Precision.HIGHEST)
    for j in range(NODES):
        part = mm(jnp.asarray(toeplitz[j].astype(ml_dtypes.bfloat16)), gated)
        result = result + coef[j][None, :] * part
    return queries * result.astype(jnp.bfloat16).astype(jnp.float32)


def solution(mesh):
    in_specs = (P(("dp", "ctx"), None), P(), P(), P())
    out_specs = P(("dp", "ctx"), None)
    return jax.shard_map(shards, mesh=mesh, in_specs=in_specs, out_specs=out_specs, check_vma=False)
```

profile of v0, /device:TPU:1, one launch (start us, length us, event | category | flops | bytes accessed | tf_op | source)
XLA Modules:
  0.0 193.2 jit_solution(17789589604658119803)
XLA Ops:
  1.0 4.9 %collective-permute-start = (bf16[6,12288]{1,0:T(8,128)(2,1)S(1)}, bf16[6,12288]{1,0:T(8,128)(2,1)S(1)}, u32[]{:S(2)}, u32[]{:S(2)}) collective-permute-start(bf16[6,12288]{1,0:T(8,128)(2,1)S(1)} %slice.92), channel_id=1, source_target_pairs={{0,4},{4,8},{8,12},{12,16},{16,20},{20,24},{24,28},{28,32},{32,36}... | collective-permute-start | bytes 442376 | tf_op jit(solution)/shard_map/ppermute | solution.py:33
  5.9 2.5 %fusion.23 = (f32[1,12288]{1,0:T(1,128)S(1)}, f32[1,12288]{1,0:T(1,128)S(1)}, f32[1,12288]{1,0:T(1,128)S(1)}, f32[1,12288]{1,0:T(1,128)S(1)}, f32[1,12288]{1,0:T...) fusion(f32[7,12288]{1,0:T(8,128)} %param.24), kind=kLoop, calls=%fused_computation.62 | loop fusion | bytes 688128 | tf_op jit(solution)/shard_map/slice | solution.py:37
  8.5 2.0 %sqrt_multiply_fusion = (f32[4096,16]{0,1:T(8,128)}, f32[4096,16]{0,1:T(8,128)}) fusion(f32[4096,16]{0,1:T(8,128)} %param.26, f32[4096,16]{0,1:T(8,128)} %param.25), kind=kLoop, calls=%fused_computation.56 | loop fusion | flops 262144 | bytes 1048576 | tf_op jit(solution)/shard_map/mul | solution.py:81
  10.4 8.6 %copy.84 = bf16[256,12288]{0,1:T(8,128)(2,1)} copy(bf16[256,12288]{1,0:T(8,128)(2,1)} %param.23) | data formatting | bytes 12582912 | tf_op args[0]
  19.9 2.8 %copy.85 = bf16[6,12288]{0,1:T(8,128)(2,1)} copy(bf16[6,12288]{1,0:T(8,128)(2,1)S(1)} %collective-permute-done) | data formatting | bytes 294912 | tf_op jit(solution)/shard_map/ppermute | solution.py:33
  22.7 36.6 %multiply_add_fusion = f32[256,12288]{0,1:T(8,128)S(1)} fusion(bf16[256,12288]{0,1:T(8,128)(2,1)} %copy.84, bf16[6,12288]{0,1:T(8,128)(2,1)} %copy.85, f32[12288]{0:T(1024)S(1)} %bitcast.87, f32[12288]{0:T(1024)S(1)} %bitcast.88, f32[12288]{0:T(1024)S(1)} %bitcast.83, f32[12288]{0:T(1024)S(1)} %bitcast.84, f32[12288]{0:T(1024)S(1)} %bitcast.85, ...), kind=kLoop, calls=%fused_computation.7 | loop fusion | flops 119537664 | bytes 19365888 | tf_op jit(solution)/shard_map/add | solution.py:37
  59.3 4.5 %copy-done = f32[256,12288]{0,1:T(8,128)} copy-done((f32[256,12288]{0,1:T(8,128)}, f32[256,12288]{0,1:T(8,128)S(1)}, u32[]{:S(2)}) %copy-start) | copy-done | bytes 12582936
  67.3 10.7 %all-to-all-start = ((f32[64,1,832]{2,1,0:T(1,128)}), f32[64,1,832]{2,1,0:T(1,128)S(1)}, u32[]{:S(2)}, u32[]{:S(2)}) async-start(f32[64,1,832]{2,1,0:T(1,128)} %reshape.19), calls=%async_computation | async-start | bytes 458752 | tf_op jit(solution)/shard_map/all_to_all | solution.py:61
  78.8 2.7 %multiply_reduce_fusion = f32[13,4096]{1,0:T(8,128)} fusion(f32[13]{0:T(128)S(1)} %copy-done.19, f32[4096,16]{0,1:T(8,128)} %get-tuple-element.104, f32[4096,16]{0,1:T(8,128)} %get-tuple-element.103), kind=kLoop, calls=%fused_computation.53 | loop fusion | flops 2502656 | bytes 737332 | tf_op jit(solution)/shard_map/reduce_sum | solution.py:82
  81.5 7.7 %all-to-all-done = f32[64,1,832]{2,1,0:T(1,128)S(1)} async-done(((f32[64,1,832]{2,1,0:T(1,128)}), f32[64,1,832]{2,1,0:T(1,128)S(1)}, u32[]{:S(2)}, u32[]{:S(2)}) %all-to-all-start) | async-done | bytes 213024 | tf_op jit(solution)/shard_map/all_to_all | solution.py:61
  89.7 2.0 %reduce = f32[64,832]{1,0:T(8,128)} reduce(f32[64,1,832]{2,1,0:T(1,128)S(1)} %all-to-all-done, f32[]{:T(128)} %broadcast.36), dimensions={1}, to_apply=%all_to_all.23.reduce_sub_computation | reduce | bytes 425988 | tf_op jit(solution)/shard_map/all_to_all | solution.py:61
  91.7 1.9 reshape.20
  93.6 2.2 %copy.89 = f32[13,64,64]{1,0,2:T(8,128)} copy(f32[13,64,64]{2,0,1:T(8,128)} %bitcast.80) | data formatting | bytes 425984 | tf_op jit(solution)/shard_map/all_to_all | solution.py:61
  95.7 2.5 %convolution_bitcast_fusion.1 = f32[64,64,16]{0,2,1:T(8,128)} fusion(f32[64,16,13]{2,1,0:T(8,128)S(1)} %copy.88, f32[13,64,64]{1,0,2:T(8,128)} %copy.89), kind=kOutput, calls=%fused_computation.55 | convolution fusion | flops 10223616 | bytes 528384 | tf_op jit(solution)/shard_map/djc,crj->dcr/dot_general | solution.py:69
  99.6 38.8 %while.13 = (s32[]{:T(128)}, f32[64,16]{0,1:T(8,128)S(1)}, f32[64,64,16]{1,2,0:T(8,128)}, f32[64,16]{0,1:T(8,128)S(1)}, f32[64,64,16]{1,2,0:T(8,128)S(1)}, /*index=5*/s32[]{:T(128)}, s32[]{:T(128)}) while((s32[]{:T(128)}, f32[64,16]{0,1:T(8,128)S(1)}, f32[64,64,16]{1,2,0:T(8,128)}, f32[64,16]{0,1:T(8,128)S(1)}, ...), condition=%wide.region_1.2_spmd.clone, body=%wide.region_0.1_spmd.clone.sunk | while | flops 4099 | bytes 29276 | solution.py:75
  139.7 1.4 convolution_bitcast_fusion
  143.6 6.3 %all-to-all-start.1 = ((f32[64,1,832]{2,1,0:T(1,128)}), f32[64,1,832]{2,1,0:T(1,128)S(1)}, u32[]{:S(2)}, u32[]{:S(2)}) async-start(f32[64,1,832]{2,1,0:T(1,128)} %reshape.21), calls=%async_computation.1 | async-start | bytes 458752 | tf_op jit(solution)/shard_map/all_to_all | solution.py:79
  149.9 2.2 %fusion.24 = (f32[1,4096]{1,0:T(1,128)S(1)}, f32[1,4096]{1,0:T(1,128)S(1)}, f32[1,4096]{1,0:T(1,128)S(1)}, f32[1,4096]{1,0:T(1,128)S(1)}, f32[1,4096]{1,0:T(1,12...) fusion(f32[13,4096]{1,0:T(8,128)} %multiply_reduce_fusion), kind=kLoop, calls=%fused_computation.63 | loop fusion | bytes 425984 | tf_op jit(solution)/shard_map/slice | solution.py:86
  152.1 8.9 %all-to-all-done.1 = f32[64,1,832]{2,1,0:T(1,128)S(1)} async-done(((f32[64,1,832]{2,1,0:T(1,128)}), f32[64,1,832]{2,1,0:T(1,128)S(1)}, u32[]{:S(2)}, u32[]{:S(2)}) %all-to-all-start.1) | async-done | bytes 213024 | tf_op jit(solution)/shard_map/all_to_all | solution.py:79
  162.7 3.6 %fusion.26 = f32[4096,256]{1,0:T(8,128)S(1)} fusion(f32[13,4096]{1,0:T(8,128)S(1)} %all_to_all.26, f32[256,13]{1,0:T(8,128)S(1)} %copy-done.2), kind=kOutput, calls=%fused_computation.66 | convolution fusion | flops 163577856 | bytes 4420608 | tf_op jit(solution)/shard_map/dot_general | solution.py:83
  166.3 1.4 fusion.17
  167.8 1.4 fusion.16
  169.2 1.4 fusion.15
  170.6 1.4 fusion.14
  172.1 1.4 fusion.13
  173.5 1.4 fusion.12
  174.9 1.4 fusion.11
  176.4 1.4 fusion.10
  177.8 1.4 fusion.9
  180.7 1.4 fusion.7
  183.5 4.0 %slice_multiply_fusion.1 = f32[256,4096]{0,1:T(8,128)} fusion(f32[256,12288]{0,1:T(8,128)} %copy-done, f32[4096,256]{1,0:T(8,128)S(1)} %fusion.6, bf16[256,4096]{0,1:T(8,128)(2,1)S(1)} %fusion.22, bf16[256,256]{1,0:T(8,128)(2,1)S(1)} %copy-done.1, f32[4096]{0:T(1024)S(1)} %bitcast.101), kind=kOutput, calls=%fused_computation.52 | convolution fusion | flops 542113792 | bytes 14827520 | tf_op jit(solution)/shard_map/dot_general | solution.py:42
  187.6 5.6 %copy.95 = f32[256,4096]{1,0:T(8,128)} copy(f32[256,4096]{0,1:T(8,128)} %slice_multiply_fusion.1) | data formatting | bytes 8388608 | tf_op jit(solution)/shard_map/mul | solution.py:87
  (192 shorter events, 54.9 us)
Async XLA Ops:
  1.0 18.9 %collective-permute-start = (bf16[6,12288]{1,0:T(8,128)(2,1)S(1)}, bf16[6,12288]{1,0:T(8,128)(2,1)S(1)}, u32[]{:S(2)}, u32[]{:S(2)}) collective-permute-start(bf16[6,12288]{1,0:T(8,128)(2,1)S(1)} %slice.92), channel_id=1, source_target_pairs={{0,4},{4,8},{8,12},{12,16},{16,20},{20,24},{24,28},{28,32},{32,36}... | collective-permute-start | bytes 442376 | tf_op jit(solution)/shard_map/ppermute | solution.py:33
  59.3 4.5 %copy-start = (f32[256,12288]{0,1:T(8,128)}, f32[256,12288]{0,1:T(8,128)S(1)}, u32[]{:S(2)}) copy-start(f32[256,12288]{0,1:T(8,128)S(1)} %multiply_add_fusion) | copy-start | bytes 37748740
  63.9 0.7 copy-start.16
  63.9 1.3 copy-start.15
  64.6 13.5 %copy-start.17 = (f32[13]{0:T(128)S(1)}, f32[13]{0:T(128)}, u32[]{:S(2)}) copy-start(f32[13]{0:T(128)} %constant.85) | copy-start | bytes 160
  64.6 13.5 %copy-start.18 = (f32[13]{0:T(128)S(1)}, f32[13]{0:T(128)}, u32[]{:S(2)}) copy-start(f32[13]{0:T(128)} %constant.87) | copy-start | bytes 160
  64.6 14.2 %copy-start.19 = (f32[13]{0:T(128)S(1)}, f32[13]{0:T(128)}, u32[]{:S(2)}) copy-start(f32[13]{0:T(128)} %constant.68.clone) | copy-start | bytes 160
  67.3 21.8 %all-to-all-start = ((f32[64,1,832]{2,1,0:T(1,128)}), f32[64,1,832]{2,1,0:T(1,128)S(1)}, u32[]{:S(2)}, u32[]{:S(2)}) async-start(f32[64,1,832]{2,1,0:T(1,128)} %reshape.19), calls=%async_computation | async-start | bytes 458752 | tf_op jit(solution)/shard_map/all_to_all | solution.py:61
  99.6 63.1 %copy-start.2 = (f32[256,13]{1,0:T(8,128)S(1)}, f32[256,13]{1,0:T(8,128)}, u32[]{:S(2)}) copy-start(f32[256,13]{1,0:T(8,128)} %constant.71.clone) | copy-start | bytes 39940
  143.6 22.7 %copy-start.14 = (bf16[256,256]{1,0:T(8,128)(2,1)S(1)}, bf16[256,256]{1,0:T(8,128)(2,1)}, u32[]{:S(2)}) copy-start(bf16[256,256]{1,0:T(8,128)(2,1)} %constant.72.clone) | copy-start | bytes 393220
  143.6 17.5 %all-to-all-start.1 = ((f32[64,1,832]{2,1,0:T(1,128)}), f32[64,1,832]{2,1,0:T(1,128)S(1)}, u32[]{:S(2)}, u32[]{:S(2)}) async-start(f32[64,1,832]{2,1,0:T(1,128)} %reshape.21), calls=%async_computation.1 | async-start | bytes 458752 | tf_op jit(solution)/shard_map/all_to_all | solution.py:79
  166.3 1.4 copy-start.13
  167.7 1.4 copy-start.12
  169.2 1.4 copy-start.11
  170.6 1.4 copy-start.10
  172.0 1.4 copy-start.9
  173.5 1.4 copy-start.8
  174.9 1.4 copy-start.7
  176.4 1.4 copy-start.6
  177.8 1.4 copy-start.5
  179.2 1.4 copy-start.4
  180.7 1.4 copy-start.3
  182.1 1.4 copy-start.1
where the time goes:
time: 194 us; the launch traced here: 193 us
  other arithmetic  84.6 us (44%)
  local copies, waits for them, and re-layouts  39.7 us (20%)
  matrix products  29.7 us (15%)
  starting transfers between devices  22 us (11%)
  waiting for transfers between devices  16.6 us (9%)
    dynamic_update_slice x64, other arithmetic, shards(): _, held = lax.scan(advance, jnp.zeros_like(states[0]), states)  38.3 us
    add x1, other arithmetic, short_filter(): total + taps[shift][None, :] * joined[lead - shift:lead - shift + rows].a...  36.6 us
    dot_general x15, matrix products, mm(): return jnp.dot(a, b, preferred_element_type=jnp.float32)  22.2 us
    unnamed x46, local copies, waits for them, and re-layouts  18.8 us
    all_to_all x1, starting transfers between devices, shards(): lax.all_to_all(moments, 'ctx', split_axis=1, concat_axis=0, tiled=True)  10.7 us
    all_to_all x1, waiting for transfers between devices, shards(): past = lax.all_to_all(past, 'ctx', split_axis=0, concat_axis=1, tiled=True)  8.92 us
    all_to_all x1, waiting for transfers between devices, shards(): lax.all_to_all(moments, 'ctx', split_axis=1, concat_axis=0, tiled=True)  7.68 us
    all_to_all x1, starting transfers between devices, shards(): past = lax.all_to_all(past, 'ctx', split_axis=0, concat_axis=1, tiled=True)  6.34 us
  transfers between devices with their start and end apart: 3, of which 2 were waited for; matrix products, arithmetic and copies ran while one was open for 10% of the time, Pallas kernels for 0%

commit v1 on v0

v1 whole, which is shorter than its diff:
```python
import functools

import jax
import jax.numpy as jnp
import ml_dtypes
import numpy as np
from jax import lax
from jax.experimental import pallas as pl
from jax.experimental.pallas import tpu as pltpu
from jax.sharding import PartitionSpec as P

F32, BF16 = jnp.float32, jnp.bfloat16
MESH = pl.DeviceIdType.MESH
NODES = 7
CHUNK = 128
GROUP = 16
TOP_RATE = 0.033
LOW_RATE = 3.0517578e-05


def chunk_basis(length):
    rates = 0.5 * TOP_RATE * (1.0 + np.cos(np.linspace(0.0, np.pi, 600)))
    rates = np.clip(rates, LOW_RATE, TOP_RATE)
    family = np.exp(-rates[:, None] * np.arange(length))
    space = np.linalg.svd(family, full_matrices=False)[2][:NODES].T
    rest, picked = space.T.copy(), []
    for _ in range(NODES):
        best = int(np.argmax((rest**2).sum(0)))
        picked.append(best)
        unit = rest[:, best] / np.linalg.norm(rest[:, best])
        rest = rest - np.outer(unit, unit @ rest)
    picked = sorted(picked)
    return picked, space @ np.linalg.inv(space[picked])


def split_pair(table):
    high = table.astype(ml_dtypes.bfloat16)
    low = (table - high.astype(np.float64)).astype(ml_dtypes.bfloat16)
    return high, low


def tables():
    nodes, basis = chunk_basis(CHUNK)
    lag = np.arange(CHUNK)[:, None] - np.arange(CHUNK)[None, :]
    local = np.where(lag[None] >= 0, basis.T[:, np.maximum(lag, 0)], 0.0)
    local = np.concatenate(list(local), 1).astype(ml_dtypes.bfloat16)
    block = np.zeros((2 * CHUNK, 16))
    for half in range(2):
        block[half * CHUNK : (half + 1) * CHUNK, 8 * half : 8 * half + NODES] = basis
    high, low = split_pair(block)
    spread = np.concatenate([high, low], 1)
    gather = np.concatenate([high.T, low.T], 0)
    return nodes, local, gather, spread


def mm(a, b):
    return jnp.dot(a, b, preferred_element_type=F32)


def lanes(start, size):
    return pl.ds(pl.multiple_of(start, 128), size)


def kernel(
    nodes, width, proj_hbm, taps, rates, weights, local, gather, spread, out_hbm,
    proj, halo, shifted, gated, queries, conv, coef, send_m, recv_m, send_t, recv_t, send_g, recv_g,
    into, outof, decay, decay_scan, plain_m, scans, carries, plain_g,
    in_sem, out_sem, halo_send, halo_recv, m_send, m_recv, t_send, t_recv, g_send, g_recv,
):
    ctx = lax.axis_index("ctx")
    peers = lax.axis_size("ctx")
    outer = peers // GROUP
    own = lax.rem(ctx, GROUP)
    row = lax.div(ctx, GROUP)
    base = row * GROUP
    after, before = lax.rem(ctx + 1, peers), lax.rem(ctx + peers - 1, peers)
    part = width // GROUP

    barrier = pltpu.get_barrier_semaphore()

    def greet(device):
        pl.semaphore_signal(barrier, inc=1, device_id={"ctx": device}, device_id_type=MESH)

    greet(after)
    greet(before)

    def greet_group(i, c):
        @pl.when(i != own)
        def _():
            greet(base + i)

        return c

    lax.fori_loop(0, GROUP, greet_group, 0)

    def greet_outer(i, c):
        @pl.when(i != row)
        def _():
            greet(i * GROUP + own)

        return c

    lax.fori_loop(0, outer, greet_outer, 0)

    wide = 512
    steps = width // wide

    def fetch(which, t):
        cols = lanes(which * width + t * wide, wide)
        return pltpu.make_async_copy(proj_hbm.at[:, cols], proj.at[:, cols], in_sem.at[which, t])

    def fetch_all(t, c):
        fetch(1, t).start()
        fetch(2, t).start()
        return c

    lax.fori_loop(0, steps, fetch_all, 0)

    def fetch_q(t, c):
        fetch(0, t).start()
        return c

    lax.fori_loop(0, steps, fetch_q, 0)

    pl.semaphore_wait(barrier, 2 + (GROUP - 1) + (outer - 1))

    rows = proj.shape[0]

    def halo_copy(n, start, size):
        return pltpu.make_async_remote_copy(
            src_ref=proj_hbm.at[pl.ds(rows - 8, 8), pl.ds(start, size)],
            dst_ref=halo.at[:, pl.ds(start, size)],
            send_sem=halo_send.at[n],
            recv_sem=halo_recv.at[n],
            device_id={"ctx": after},
            device_id_type=MESH,
        )

    halo_kv = halo_copy(0, width, 2 * width)
    halo_q = halo_copy(1, 0, width)
    halo_kv.start()
    halo_q.start()

    def amplitude(rate, weight):
        x = 2.0 * rate
        series = 1.0 - x * (0.5 - x * (1 / 6 - x * (1 / 24 - x * (1 / 120 - x * (1 / 720)))))
        return weight * jnp.sqrt(x * series)

    def prepare(t, c):
        cols = lanes(t * wide, wide)
        rate = rates[:, cols]
        amp = amplitude(rate, weights[:, cols])
        for j, n in enumerate(nodes):
            coef[j : j + 1, cols] = jnp.sum(amp * jnp.exp(rate * (-float(n))), axis=0, keepdims=True)
        return c

    lax.fori_loop(0, steps, prepare, 0)

    mine = lanes(own * part, part)
    rate = rates[:, mine]
    amp = amplitude(rate, weights[:, mine])
    for j, n in enumerate(nodes):
        into[16 * j : 16 * j + 16, :] = jnp.exp(rate * (-float(CHUNK - 1 - n)))
        outof[16 * j : 16 * j + 16, :] = amp * jnp.exp(rate * (-float(1 + n)))
    sub = lax.broadcasted_iota(jnp.int32, (8, part), 0)
    far = (sub + 1).astype(F32) * (-float(CHUNK))
    for r in range(16):
        one = jnp.broadcast_to(rate[r : r + 1], (8, part))
        decay[r] = jnp.exp(one * far)
        for k, hop in enumerate((1, 2, 4)):
            decay_scan[3 * r + k] = jnp.where(sub >= hop, jnp.exp(one * (-float(CHUNK * hop))), 0.0)

    halo_kv.wait()
    first = jnp.where(ctx == 0, 0.0, 1.0)

    def lay(slot, start):
        cols = lanes(start, 128)
        shifted[slot, 0:8, :] = halo[:, cols].astype(F32) * first
        for k in range(rows // 16):
            shifted[slot, 8 + 16 * k : 24 + 16 * k, :] = proj[16 * k : 16 * k + 16, cols].astype(F32)

    def tap_rows(start):
        cols = lanes(start, 128)
        block = taps[:, cols]
        return [jnp.broadcast_to(block[j : j + 1], (8, 128)) for j in range(taps.shape[0])]

    def filtered(slot, k, weights_j):
        total = None
        for j, w in enumerate(weights_j):
            term = shifted[slot, 8 + 8 * k - j : 16 + 8 * k - j, :] * w
            total = term if total is None else total + term
        return total

    def moment_copy(o):
        return pltpu.make_async_remote_copy(
            src_ref=send_m.at[o],
            dst_ref=recv_m.at[own],
            send_sem=m_send.at[o],
            recv_sem=m_recv.at[own],
            device_id={"ctx": base + o},
            device_id_type=MESH,
        )

    def moments(o):
        both = mm(gather[...], gated[:, lanes(o * part, part)])
        return (both[:16] + both[16:]).astype(BF16)

    def send_moments(o, value):
        send_m[o] = value

        @pl.when(o == own)
        def _():
            recv_m[own] = value

        @pl.when(o != own)
        def _():
            moment_copy(o).start()

    def gate(i, c):
        @pl.when(lax.rem(i, wide // part) == 0)
        def _():
            t = lax.div(i, wide // part)
            fetch(1, t).wait()
            fetch(2, t).wait()

        last = jnp.maximum(i - 1, 0)
        ready = moments(last)
        for h in range(part // 128):
            at = i * part + 128 * h
            lay(2 * h, width + at)
            lay(2 * h + 1, 2 * width + at)
            tk, tv = tap_rows(width + at), tap_rows(2 * width + at)
            for k in range(rows // 16):
                pair = [filtered(2 * h, 2 * k + b, tk) * filtered(2 * h + 1, 2 * k + b, tv) for b in range(2)]
                gated[16 * k : 16 * k + 16, lanes(at, 128)] = jnp.concatenate(pair, 0).astype(BF16)

        @pl.when(i > 0)
        def _():
            send_moments(last, ready)

        return c

    lax.fori_loop(0, GROUP, gate, 0)
    send_moments(GROUP - 1, moments(GROUP - 1))
    halo_q.wait()

    def total_copy(x):
        return pltpu.make_async_remote_copy(
            src_ref=send_t,
            dst_ref=recv_t.at[row],
            send_sem=t_send.at[x],
            recv_sem=t_recv.at[row],
            device_id={"ctx": x * GROUP + own},
            device_id_type=MESH,
        )

    def total_arrival(x):
        return pltpu.make_async_remote_copy(
            src_ref=send_t,
            dst_ref=recv_t.at[x],
            send_sem=t_send.at[x],
            recv_sem=t_recv.at[x],
            device_id={"ctx": x * GROUP + own},
            device_id_type=MESH,
        )

    def moment_arrival(s):
        return pltpu.make_async_remote_copy(
            src_ref=send_m.at[s],
            dst_ref=recv_m.at[s],
            send_sem=m_send.at[s],
            recv_sem=m_recv.at[s],
            device_id={"ctx": base + s},
            device_id_type=MESH,
        )

    def past_copy(d):
        return pltpu.make_async_remote_copy(
            src_ref=send_g.at[d],
            dst_ref=recv_g.at[own],
            send_sem=g_send.at[d],
            recv_sem=g_recv.at[own],
            device_id={"ctx": base + d},
            device_id_type=MESH,
        )

    def past_arrival(s):
        return pltpu.make_async_remote_copy(
            src_ref=send_g.at[s],
            dst_ref=recv_g.at[s],
            send_sem=g_send.at[s],
            recv_sem=g_recv.at[s],
            device_id={"ctx": base + s},
            device_id_type=MESH,
        )

    halves = part // 128
    sub128 = lax.broadcasted_iota(jnp.int32, (8, 128), 0)

    def gather_states():
        def arrive(s, c):
            @pl.when(s != own)
            def _():
                moment_arrival(s).wait()

            return c

        lax.fori_loop(0, GROUP, arrive, 0)
        for s in range(GROUP):
            block = recv_m[s].astype(F32)
            for h in range(halves):
                plain_m[h, 16 * s : 16 * s + 16, :] = block[:, 128 * h : 128 * h + 128]

        for h in range(halves):
            cols = slice(128 * h, 128 * h + 128)

            def scan_group(g, c, h=h, cols=cols):
                m = [plain_m[h, pl.ds(g * 64 + j, 8, stride=8), :] for j in range(NODES)]
                for r in range(16):
                    state = None
                    for j in range(NODES):
                        term = m[j] * into[16 * j + r : 16 * j + r + 1, cols]
                        state = term if state is None else state + term
                    for k, hop in enumerate((1, 2, 4)):
                        state = state + decay_scan[3 * r + k, :, cols] * pltpu.roll(state, hop, 0)
                    scans[h, pl.ds(pl.multiple_of(r * 32 + 8 * g, 8), 8), :] = state
                return c

            lax.fori_loop(0, 4, scan_group, 0)
            step8 = jnp.exp(rates[:, lanes(own * part + 128 * h, 128)] * (-float(8 * CHUNK)))
            total = scans[h, pl.ds(7, 16, stride=32), :]
            for g in range(1, 4):
                total = total * step8 + scans[h, pl.ds(8 * g + 7, 16, stride=32), :]
            send_t[:, cols] = total

        def send(x, c):
            @pl.when(x != row)
            def _():
                total_copy(x).start()

            return c

        lax.fori_loop(0, outer, send, 0)

    def spread_states():
        def arrive(x, c):
            @pl.when(x != row)
            def _():
                total_arrival(x).wait()

            return c

        lax.fori_loop(0, outer, arrive, 0)
        for h in range(halves):
            cols = slice(128 * h, 128 * h + 128)
            rate = rates[:, lanes(own * part + 128 * h, 128)]
            step8 = jnp.exp(rate * (-float(8 * CHUNK)))
            step32 = jnp.exp(rate * (-float(32 * CHUNK)))
            held = jnp.zeros((16, 128), F32)
            for x in range(outer - 1):
                held = jnp.where(x < row, held * step32 + recv_t[x, :, cols], held)
            for g in range(4):
                carries[h, 16 * g : 16 * g + 16, :] = held
                held = held * step8 + scans[h, pl.ds(8 * g + 7, 16, stride=32), :]

            def spread_group(g, c, h=h, cols=cols):
                states = []
                for r in range(16):
                    carry = jnp.broadcast_to(carries[h, pl.ds(16 * g + r, 1), :], (8, 128))
                    full = scans[h, pl.ds(pl.multiple_of(r * 32 + 8 * g, 8), 8), :] + decay[r, :, cols] * carry
                    states.append(jnp.where(sub128 == 0, carry, pltpu.roll(full, 1, 0)))
                for j in range(NODES):
                    past = None
                    for r in range(16):
                        term = states[r] * outof[16 * j + r : 16 * j + r + 1, cols]
                        past = term if past is None else past + term
                    plain_g[h, pl.ds(g * 64 + j, 8, stride=8), :] = past
                plain_g[h, pl.ds(g * 64 + NODES, 8, stride=8), :] = jnp.zeros((8, 128), F32)
                return c

            lax.fori_loop(0, 4, spread_group, 0)
        for d in range(GROUP):
            for h in range(halves):
                send_g[d, :, 128 * h : 128 * h + 128] = plain_g[h, 16 * d : 16 * d + 16, :].astype(BF16)
        recv_g[own] = send_g[own]

        def send(d, c):
            @pl.when(d != own)
            def _():
                past_copy(d).start()

            return c

        lax.fori_loop(0, GROUP, send, 0)

    def within(t, c):
        fetch(0, t).wait()

        @pl.when(t == 2)
        def _():
            gather_states()

        @pl.when(t == 5)
        def _():
            spread_states()

        for piece in range(2):
            cols = lanes(t * wide + 256 * piece, 256)
            scale = coef[:, cols].astype(BF16)
            for half in range(2):
                tokens = slice(half * CHUNK, (half + 1) * CHUNK)
                field = gated[tokens, cols]
                stacked = jnp.concatenate([field * scale[j : j + 1] for j in range(NODES)], 0)
                result = mm(local[...], stacked)
                at = t * wide + 256 * piece + 128 * half
                slot = 2 * piece + half
                lay(slot, at)
                tq = tap_rows(at)
                for k in range(rows // 8):
                    queries[8 * k : 8 * k + 8, lanes(at, 128)] = filtered(slot, k, tq)
                conv[tokens, cols] = result
        return c

    lax.fori_loop(0, steps, within, 0)

    def store(t):
        cols = lanes(t * wide, wide)
        return pltpu.make_async_copy(queries.at[:, cols], out_hbm.at[:, cols], out_sem.at[t])

    def finish(t, c):
        per = wide // part
        for b in range(per):
            o = per * t + b

            @pl.when(o != own)
            def _(o=o):
                past_arrival(o).wait()

        for b in range(per):
            o = per * t + b
            cols = lanes(o * part, part)
            past = recv_g[o]
            result = mm(spread[...], jnp.concatenate([past, past], 0))
            queries[:, cols] = queries[:, cols] * (conv[:, cols] + result)
        store(t).start()
        return c

    lax.fori_loop(0, steps, finish, 0)

    def close_out(t, c):
        store(t).wait()
        return c

    lax.fori_loop(0, steps, close_out, 0)


def shards(projected, taps, decays, residues):
    rows = projected.shape[0]
    width = taps.shape[1] // 3
    part = width // GROUP
    outer = lax.axis_size("ctx") // GROUP
    nodes, local, gather, spread = tables()
    turned = jnp.concatenate([decays, residues], 1).T
    rates, weights = turned[:16], turned[16:]
    vmem = pl.BlockSpec(memory_space=pltpu.VMEM)
    hbm = pl.BlockSpec(memory_space=pl.ANY)
    dma = pltpu.SemaphoreType.DMA
    steps = width // 512
    return pl.pallas_call(
        functools.partial(kernel, nodes, width),
        out_shape=jax.ShapeDtypeStruct((rows, width), F32),
        in_specs=[hbm, vmem, vmem, vmem, vmem, vmem, vmem],
        out_specs=hbm,
        scratch_shapes=[
            pltpu.VMEM((rows, 3 * width), BF16),
            pltpu.VMEM((8, 3 * width), BF16),
            pltpu.VMEM((4, rows + 8, 128), F32),
            pltpu.VMEM((rows, width), BF16),
            pltpu.VMEM((rows, width), F32),
            pltpu.VMEM((rows, width), F32),
            pltpu.VMEM((8, width), F32),
            pltpu.VMEM((GROUP, 16, part), BF16),
            pltpu.VMEM((GROUP, 16, part), BF16),
            pltpu.VMEM((16, part), F32),
            pltpu.VMEM((outer, 16, part), F32),
            pltpu.VMEM((GROUP, 16, part), BF16),
            pltpu.VMEM((GROUP, 16, part), BF16),
            pltpu.VMEM((16 * NODES, part), F32),
            pltpu.VMEM((16 * NODES, part), F32),
            pltpu.VMEM((16, 8, part), F32),
            pltpu.VMEM((48, 8, part), F32),
            pltpu.VMEM((part // 128, 256, 128), F32),
            pltpu.VMEM((part // 128, 512, 128), F32),
            pltpu.VMEM((part // 128, 64, 128), F32),
            pltpu.VMEM((part // 128, 256, 128), F32),
            dma((3, steps)), dma((steps,)),
            dma((2,)), dma((2,)),
            dma((GROUP,)), dma((GROUP,)),
            dma((outer,)), dma((outer,)),
            dma((GROUP,)), dma((GROUP,)),
        ],
        compiler_params=pltpu.CompilerParams(
            collective_id=0, has_side_effects=True, vmem_limit_bytes=48 * 2**20
        ),
        name="hyena",
    )(projected, taps, rates, weights, jnp.asarray(local), jnp.asarray(gather), jnp.asarray(spread))


def solution(mesh):
    in_specs = (P(("dp", "ctx"), None), P(), P(), P())
    out_specs = P(("dp", "ctx"), None)
    return jax.shard_map(shards, mesh=mesh, in_specs=in_specs, out_specs=out_specs, check_vma=False)
```

time: 194 us -> 42.6 us (0.22)
  other arithmetic: 84.6 us -> 1.06 us
  Pallas kernels: 0 us -> 35.7 us
  local copies, waits for them, and re-layouts: 39.7 us -> 5.54 us
  matrix products: 29.7 us -> 0 us
  starting transfers between devices: 22 us -> 0 us
  waiting for transfers between devices: 16.6 us -> 0 us
    dynamic_update_slice x64 -> x0, other arithmetic: 38.3 us -> none  [shards(): _, held = lax.scan(advance, jnp.zeros_like(states[0]), states)]
    add x65 -> x0, other arithmetic: 37 us -> none  [the longest x1 36.6 us: short_filter(): total + taps[shift][None, :] * joined[lead - shift:lead - shift + rows].a...]
    pallas_call x0 -> x1, Pallas kernels: none -> 35.7 us  [shards(): pl.pallas_call(functools.partial(kernel, nodes, width), out_shape=jax.Sha...]
    dot_general x18 -> x0, matrix products: 29.7 us -> none  [the longest x15 22.2 us: mm(): return jnp.dot(a, b, preferred_element_type=jnp.float32)]
    all_to_all x2 -> x0, starting transfers between devices: 17 us -> none  [the longest x1 10.7 us: shards(): lax.all_to_all(moments, 'ctx', split_axis=1, concat_axis=0, tiled=True)]
    all_to_all x2 -> x0, waiting for transfers between devices: 16.6 us -> none  [the longest x1 8.92 us: shards(): past = lax.all_to_all(past, 'ctx', split_axis=0, concat_axis=1, tiled=True)]
    unnamed x46 -> x9, local copies, waits for them, and re-layouts: 18.8 us -> 5.5 us
    mul x2 -> x0, local copies, waits for them, and re-layouts: 5.87 us -> none  [the longest x1 5.59 us: shards(): return queries * result.astype(jnp.bfloat16).astype(jnp.float32)]
  transfers between devices with their start and end apart: 3 -> 0, of which waited for: 2 -> 0; matrix products, arithmetic and copies ran while one was open for 10% -> 0% of each run, Pallas kernels for 0% -> 0%
where the time goes in v1:
time: 42.6 us; the launch traced here: 42.3 us
  Pallas kernels  35.7 us (84%)
  local copies, waits for them, and re-layouts  5.54 us (13%)
  other arithmetic  1.06 us (2%)
    pallas_call x1, Pallas kernels, shards(): pl.pallas_call(functools.partial(kernel, nodes, width), out_shape=jax.Sha...  35.7 us
    unnamed x9, local copies, waits for them, and re-layouts  5.5 us
    transpose x1, other arithmetic, shards(): turned = jnp.concatenate([decays, residues], 1).T  1.06 us

profile of v1, /device:TPU:1, one launch (start us, length us, event | category | flops | bytes accessed | tf_op | source)
XLA Modules:
  0.0 42.3 jit_solution(13868551667847837849)
XLA Ops:
  0.0 1.1 %maximum_bitcast_fusion = f32[32,4096]{1,0:T(8,128)S(1)} fusion(f32[4096,16]{0,1:T(8,128)} %param.10, f32[4096,16]{0,1:T(8,128)} %param.9), kind=kLoop, calls=%fused_computation | loop fusion | flops 131072 | bytes 1048576 | tf_op jit(solution)/shard_map/transpose | solution.py:463
  1.1 0.0 copy-start
  1.1 1.0 %copy-done = f32[7,12288]{1,0:T(8,128)S(1)} copy-done((f32[7,12288]{1,0:T(8,128)S(1)}, f32[7,12288]{1,0:T(8,128)}, u32[]{:S(2)}) %copy-start) | copy-done | bytes 344088
  2.1 0.0 copy-start.1
  2.1 0.9 %copy-done.1 = bf16[128,896]{1,0:T(8,128)(2,1)S(1)} copy-done((bf16[128,896]{1,0:T(8,128)(2,1)S(1)}, bf16[128,896]{1,0:T(8,128)(2,1)}, u32[]{:S(2)}) %copy-start.1) | copy-done | bytes 229400
  3.1 0.0 copy-start.2
  3.1 0.8 %copy-done.2 = bf16[256,32]{1,0:T(8,128)(2,1)S(1)} copy-done((bf16[256,32]{1,0:T(8,128)(2,1)S(1)}, bf16[256,32]{1,0:T(8,128)(2,1)}, u32[]{:S(2)}) %copy-start.2) | copy-done | bytes 16408
  3.9 0.0 copy-start.3
  3.9 0.7 %copy-done.3 = bf16[32,256]{1,0:T(8,128)(2,1)S(1)} copy-done((bf16[32,256]{1,0:T(8,128)(2,1)S(1)}, bf16[32,256]{1,0:T(8,128)(2,1)}, u32[]{:S(2)}) %copy-start.3) | copy-done | bytes 16408
  4.6 35.7 %hyena.1 = f32[256,4096]{1,0:T(8,128)S(1)} custom-call(bf16[256,12288]{1,0:T(8,128)(2,1)} %proj_hbm.1, f32[7,12288]{1,0:T(8,128)S(1)} %copy-done, f32[16,4096]{1,0:T(8,128)S(1)} %get-tuple-element.6.rates, f32[16,4096]{1,0:T(8,128)S(1)} %get-tuple-element.5.weights, bf16[128,896]{1,0:T(8,128)(2,1)S(1)} %copy-done.1, bf16[32,256]{1,0:T(8,128)(2,1)S(1)} %copy-done.3, ...), custom_call_target="tpu_custom_call" | custom-call | tf_op jit(solution)/shard_map/hyena/pallas_call | solution.py:469
  40.3 2.0 %copy.9 = f32[256,4096]{1,0:T(8,128)} copy(f32[256,4096]{1,0:T(8,128)S(1)} %hyena.1) | data formatting | bytes 8388608
  (1 shorter events, 0.0 us)
Async XLA Ops:
  1.1 1.0 %copy-start = (f32[7,12288]{1,0:T(8,128)S(1)}, f32[7,12288]{1,0:T(8,128)}, u32[]{:S(2)}) copy-start(f32[7,12288]{1,0:T(8,128)} %taps.1) | copy-start | bytes 1032196
  2.1 0.9 %copy-start.1 = (bf16[128,896]{1,0:T(8,128)(2,1)S(1)}, bf16[128,896]{1,0:T(8,128)(2,1)}, u32[]{:S(2)}) copy-start(bf16[128,896]{1,0:T(8,128)(2,1)} %constant.6.clone.local) | copy-start | bytes 688132
  3.1 0.8 %copy-start.2 = (bf16[256,32]{1,0:T(8,128)(2,1)S(1)}, bf16[256,32]{1,0:T(8,128)(2,1)}, u32[]{:S(2)}) copy-start(bf16[256,32]{1,0:T(8,128)(2,1)} %constant.8.clone.spread) | copy-start | bytes 49156
  3.9 0.7 %copy-start.3 = (bf16[32,256]{1,0:T(8,128)(2,1)S(1)}, bf16[32,256]{1,0:T(8,128)(2,1)}, u32[]{:S(2)}) copy-start(bf16[32,256]{1,0:T(8,128)(2,1)} %constant.7.clone.gather) | copy-start | bytes 49156

commit v2 on v1

--- a/solution.py
+++ b/solution.py
@@ -62,10 +62,11 @@
 
 
 def kernel(
-    nodes, width, proj_hbm, taps, rates, weights, local, gather, spread, out_hbm,
-    proj, halo, shifted, gated, queries, conv, coef, send_m, recv_m, send_t, recv_t, send_g, recv_g,
+    nodes, width, proj_hbm, taps_hbm, rates_hbm, weights_hbm, local_hbm, gather_hbm, spread_hbm, queries,
+    taps, rates, weights, local, gather, spread,
+    proj, halo, shifted, gated, conv, coef, send_m, recv_m, send_t, recv_t, send_g, recv_g,
     into, outof, decay, decay_scan, plain_m, scans, carries, plain_g,
-    in_sem, out_sem, halo_send, halo_recv, m_send, m_recv, t_send, t_recv, g_send, g_recv,
+    small_sem, in_sem, halo_send, halo_recv, m_send, m_recv, t_send, t_recv, g_send, g_recv,
 ):
     ctx = lax.axis_index("ctx")
     peers = lax.axis_size("ctx")
@@ -102,6 +103,13 @@
 
     lax.fori_loop(0, outer, greet_outer, 0)
 
+    pairs = (
+        (rates_hbm, rates), (weights_hbm, weights), (taps_hbm, taps),
+        (gather_hbm, gather), (local_hbm, local), (spread_hbm, spread),
+    )
+    small = [pltpu.make_async_copy(a, b, small_sem.at[n]) for n, (a, b) in enumerate(pairs)]
+    small[2].start()
+
     wide = 512
     steps = width // wide
 
@@ -120,9 +128,9 @@
         fetch(0, t).start()
         return c
 
+    for n in (3, 0, 1, 4, 5):
+        small[n].start()
     lax.fori_loop(0, steps, fetch_q, 0)
-
-    pl.semaphore_wait(barrier, 2 + (GROUP - 1) + (outer - 1))
 
     rows = proj.shape[0]
 
@@ -136,9 +144,12 @@
             device_id_type=MESH,
         )
 
-    halo_kv = halo_copy(0, width, 2 * width)
-    halo_q = halo_copy(1, 0, width)
-    halo_kv.start()
+    quarter = width // 4
+    halo_q = halo_copy(8, 0, width)
+    halo_kv = [halo_copy(n, (1 + n % 2) * width + (n // 2) * quarter, quarter) for n in range(8)]
+    pl.semaphore_wait(barrier, 2 + (GROUP - 1) + (outer - 1))
+    for piece in halo_kv:
+        piece.start()
     halo_q.start()
 
     def amplitude(rate, weight):
@@ -146,37 +157,37 @@
         series = 1.0 - x * (0.5 - x * (1 / 6 - x * (1 / 24 - x * (1 / 120 - x * (1 / 720)))))
         return weight * jnp.sqrt(x * series)
 
-    def prepare(t, c):
+    def prepare(t):
         cols = lanes(t * wide, wide)
         rate = rates[:, cols]
         amp = amplitude(rate, weights[:, cols])
         for j, n in enumerate(nodes):
             coef[j : j + 1, cols] = jnp.sum(amp * jnp.exp(rate * (-float(n))), axis=0, keepdims=True)
-        return c
-
-    lax.fori_loop(0, steps, prepare, 0)
-
-    mine = lanes(own * part, part)
-    rate = rates[:, mine]
-    amp = amplitude(rate, weights[:, mine])
-    for j, n in enumerate(nodes):
-        into[16 * j : 16 * j + 16, :] = jnp.exp(rate * (-float(CHUNK - 1 - n)))
-        outof[16 * j : 16 * j + 16, :] = amp * jnp.exp(rate * (-float(1 + n)))
-    sub = lax.broadcasted_iota(jnp.int32, (8, part), 0)
-    far = (sub + 1).astype(F32) * (-float(CHUNK))
-    for r in range(16):
-        one = jnp.broadcast_to(rate[r : r + 1], (8, part))
-        decay[r] = jnp.exp(one * far)
-        for k, hop in enumerate((1, 2, 4)):
-            decay_scan[3 * r + k] = jnp.where(sub >= hop, jnp.exp(one * (-float(CHUNK * hop))), 0.0)
-
-    halo_kv.wait()
-    first = jnp.where(ctx == 0, 0.0, 1.0)
-
-    def lay(slot, start):
+
+
+    def owner_tables():
+        mine = lanes(own * part, part)
+        rate = rates[:, mine]
+        amp = amplitude(rate, weights[:, mine])
+        for j, n in enumerate(nodes):
+            into[16 * j : 16 * j + 16, :] = jnp.exp(rate * (-float(CHUNK - 1 - n)))
+            outof[16 * j : 16 * j + 16, :] = amp * jnp.exp(rate * (-float(1 + n)))
+        sub = lax.broadcasted_iota(jnp.int32, (8, part), 0)
+        far = (sub + 1).astype(F32) * (-float(CHUNK))
+        for r in range(16):
+            one = jnp.broadcast_to(rate[r : r + 1], (8, part))
+            decay[r] = jnp.exp(one * far)
+            for k, hop in enumerate((1, 2, 4)):
+                decay_scan[3 * r + k] = jnp.where(sub >= hop, jnp.exp(one * (-float(CHUNK * hop))), 0.0)
+
+    small[2].wait()
+    small[3].wait()
+
+    def lay(slot, start, edge):
         cols = lanes(start, 128)
-        shifted[slot, 0:8, :] = halo[:, cols].astype(F32) * first
-        for k in range(rows // 16):
+        if edge:
+            shifted[slot, 0:8, :] = jnp.where(ctx == 0, 0.0, halo[:, cols].astype(F32))
+        for k in range(1 if edge == "only" else rows // 16):
             shifted[slot, 8 + 16 * k : 24 + 16 * k, :] = proj[16 * k : 16 * k + 16, cols].astype(F32)
 
     def tap_rows(start):
@@ -216,6 +227,20 @@
         def _():
             moment_copy(o).start()
 
+    blocks = part // 128
+
+    def edge_gate(o):
+        for h in range(blocks):
+            at = o * part + 128 * h
+            lay(2 * blocks + 2 * h, width + at, "only")
+            lay(2 * blocks + 2 * h + 1, 2 * width + at, "only")
+            tk, tv = tap_rows(width + at), tap_rows(2 * width + at)
+            both = filtered(2 * blocks + 2 * h, 0, tk) * filtered(2 * blocks + 2 * h + 1, 0, tv)
+            gated[0:8, lanes(at, 128)] = both.astype(BF16)
+
+    lag = 6
+    per_quarter = quarter // part
+
     def gate(i, c):
         @pl.when(lax.rem(i, wide // part) == 0)
         def _():
@@ -223,25 +248,52 @@
             fetch(1, t).wait()
             fetch(2, t).wait()
 
-        last = jnp.maximum(i - 1, 0)
-        ready = moments(last)
-        for h in range(part // 128):
+        @pl.when(i == 3)
+        def _():
+            small[0].wait()
+            small[1].wait()
+            owner_tables()
+
+        for n in range(4):
+            if lag + n * per_quarter < GROUP:
+
+                @pl.when(i == lag + n * per_quarter)
+                def _(n=n):
+                    halo_kv[2 * n].wait()
+                    halo_kv[2 * n + 1].wait()
+
+        @pl.when(i >= lag)
+        def _():
+            edge_gate(i - lag)
+            send_moments(i - lag, moments(i - lag))
+
+        for h in range(blocks):
             at = i * part + 128 * h
-            lay(2 * h, width + at)
-            lay(2 * h + 1, 2 * width + at)
+            lay(2 * h, width + at, None)
+            lay(2 * h + 1, 2 * width + at, None)
             tk, tv = tap_rows(width + at), tap_rows(2 * width + at)
             for k in range(rows // 16):
-                pair = [filtered(2 * h, 2 * k + b, tk) * filtered(2 * h + 1, 2 * k + b, tv) for b in range(2)]
+                pair = [
+                    filtered(2 * h, 2 * k + b, tk) * filtered(2 * h + 1, 2 * k + b, tv)
+                    if k + b > 0
+                    else jnp.zeros((8, 128), F32)
+                    for b in range(2)
+                ]
                 gated[16 * k : 16 * k + 16, lanes(at, 128)] = jnp.concatenate(pair, 0).astype(BF16)
-
-        @pl.when(i > 0)
-        def _():
-            send_moments(last, ready)
-
         return c
 
     lax.fori_loop(0, GROUP, gate, 0)
-    send_moments(GROUP - 1, moments(GROUP - 1))
+
+    for n in range(4):
+        if lag + n * per_quarter >= GROUP:
+            halo_kv[2 * n].wait()
+            halo_kv[2 * n + 1].wait()
+    for o in range(GROUP - lag, GROUP):
+        edge_gate(o)
+    for o in range(GROUP - lag, GROUP):
+        send_moments(o, moments(o))
+    small[4].wait()
+    small[5].wait()
     halo_q.wait()
 
     def total_copy(x):
@@ -363,7 +415,10 @@
                 carries[h, 16 * g : 16 * g + 16, :] = held
                 held = held * step8 + scans[h, pl.ds(8 * g + 7, 16, stride=32), :]
 
-            def spread_group(g, c, h=h, cols=cols):
+        def spread_group(n, c):
+            g = lax.rem(n + lax.div(own, 4), 4)
+            for h in range(halves):
+                cols = slice(128 * h, 128 * h + 128)
                 states = []
                 for r in range(16):
                     carry = jnp.broadcast_to(carries[h, pl.ds(16 * g + r, 1), :], (8, 128))
@@ -376,34 +431,42 @@
                         past = term if past is None else past + term
                     plain_g[h, pl.ds(g * 64 + j, 8, stride=8), :] = past
                 plain_g[h, pl.ds(g * 64 + NODES, 8, stride=8), :] = jnp.zeros((8, 128), F32)
+            for b in range(4):
+                d = 4 * g + b
+                for h in range(halves):
+                    block = plain_g[h, pl.ds(pl.multiple_of(16 * d, 16), 16), :]
+                    send_g[d, :, 128 * h : 128 * h + 128] = block.astype(BF16)
+
+            def send(b, c):
+                d = 4 * g + lax.rem(b + own, 4)
+
+                @pl.when(d == own)
+                def _():
+                    recv_g[own] = send_g[d]
+
+                @pl.when(d != own)
+                def _():
+                    past_copy(d).start()
+
                 return c
 
-            lax.fori_loop(0, 4, spread_group, 0)
-        for d in range(GROUP):
-            for h in range(halves):
-                send_g[d, :, 128 * h : 128 * h + 128] = plain_g[h, 16 * d : 16 * d + 16, :].astype(BF16)
-        recv_g[own] = send_g[own]
-
-        def send(d, c):
-            @pl.when(d != own)
-            def _():
-                past_copy(d).start()
-
+            lax.fori_loop(0, 4, send, 0)
             return c
 
-        lax.fori_loop(0, GROUP, send, 0)
+        lax.fori_loop(0, 4, spread_group, 0)
 
     def within(t, c):
         fetch(0, t).wait()
 
-        @pl.when(t == 2)
+        @pl.when(t == 0)
         def _():
             gather_states()
 
-        @pl.when(t == 5)
+        @pl.when(t == 3)
         def _():
             spread_states()
 
+        prepare(t)
         for piece in range(2):
             cols = lanes(t * wide + 256 * piece, 256)
             scale = coef[:, cols].astype(BF16)
@@ -414,7 +477,7 @@
                 result = mm(local[...], stacked)
                 at = t * wide + 256 * piece + 128 * half
                 slot = 2 * piece + half
-                lay(slot, at)
+                lay(slot, at, "all")
                 tq = tap_rows(at)
                 for k in range(rows // 8):
                     queries[8 * k : 8 * k + 8, lanes(at, 128)] = filtered(slot, k, tq)
@@ -423,10 +486,6 @@
 
     lax.fori_loop(0, steps, within, 0)
 
-    def store(t):
-        cols = lanes(t * wide, wide)
-        return pltpu.make_async_copy(queries.at[:, cols], out_hbm.at[:, cols], out_sem.at[t])
-
     def finish(t, c):
         per = wide // part
         for b in range(per):
@@ -440,18 +499,14 @@
             o = per * t + b
             cols = lanes(o * part, part)
             past = recv_g[o]
-            result = mm(spread[...], jnp.concatenate([past, past], 0))
-            queries[:, cols] = queries[:, cols] * (conv[:, cols] + result)
-        store(t).start()
+            past = jnp.concatenate([past, past], 0)
+            for p in range(rows // CHUNK):
+                tokens = slice(p * CHUNK, (p + 1) * CHUNK)
+                result = mm(spread[tokens, :], past)
+                queries[tokens, cols] = queries[tokens, cols] * (conv[tokens, cols] + result)
         return c
 
     lax.fori_loop(0, steps, finish, 0)
-
-    def close_out(t, c):
-        store(t).wait()
-        return c
-
-    lax.fori_loop(0, steps, close_out, 0)
 
 
 def shards(projected, taps, decays, residues):
@@ -462,21 +517,25 @@
     nodes, local, gather, spread = tables()
     turned = jnp.concatenate([decays, residues], 1).T
     rates, weights = turned[:16], turned[16:]
-    vmem = pl.BlockSpec(memory_space=pltpu.VMEM)
-    hbm = pl.BlockSpec(memory_space=pl.ANY)
+    hbm = pl.BlockSpec(memory_space=pltpu.HBM)
     dma = pltpu.SemaphoreType.DMA
     steps = width // 512
     return pl.pallas_call(
         functools.partial(kernel, nodes, width),
-        out_shape=jax.ShapeDtypeStruct((rows, width), F32),
-        in_specs=[hbm, vmem, vmem, vmem, vmem, vmem, vmem],
-        out_specs=hbm,
+        out_shape=pltpu.VMEM((rows, width), F32),
+        in_specs=[hbm] * 7,
+        out_specs=pl.BlockSpec(memory_space=pltpu.VMEM),
         scratch_shapes=[
+            pltpu.VMEM(taps.shape, F32),
+            pltpu.VMEM(rates.shape, F32),
+            pltpu.VMEM(weights.shape, F32),
+            pltpu.VMEM(local.shape, BF16),
+            pltpu.VMEM(gather.shape, BF16),
+            pltpu.VMEM(spread.shape, BF16),
             pltpu.VMEM((rows, 3 * width), BF16),
             pltpu.VMEM((8, 3 * width), BF16),
-            pltpu.VMEM((4, rows + 8, 128), F32),
+            pltpu.VMEM((8, rows + 8, 128), F32),
             pltpu.VMEM((rows, width), BF16),
-            pltpu.VMEM((rows, width), F32),
             pltpu.VMEM((rows, width), F32),
             pltpu.VMEM((8, width), F32),
             pltpu.VMEM((GROUP, 16, part), BF16),
@@ -493,14 +552,14 @@
             pltpu.VMEM((part // 128, 512, 128), F32),
             pltpu.VMEM((part // 128, 64, 128), F32),
             pltpu.VMEM((part // 128, 256, 128), F32),
-            dma((3, steps)), dma((steps,)),
-            dma((2,)), dma((2,)),
+            dma((6,)), dma((3, steps)),
+            dma((9,)), dma((9,)),
             dma((GROUP,)), dma((GROUP,)),
             dma((outer,)), dma((outer,)),
             dma((GROUP,)), dma((GROUP,)),
         ],
         compiler_params=pltpu.CompilerParams(
-            collective_id=0, has_side_effects=True, vmem_limit_bytes=48 * 2**20
+            collective_id=0, has_side_effects=True, vmem_limit_bytes=60800 * 2**10
         ),
         name="hyena",
     )(projected, taps, rates, weights, jnp.asarray(local), jnp.asarray(gather), jnp.asarray(spread))

time: 42.6 us -> 37.6 us (0.88)
  local copies, waits for them, and re-layouts: 5.54 us -> 2.83 us
  Pallas kernels: 35.7 us -> 33.6 us
    unnamed x9 -> x1, local copies, waits for them, and re-layouts: 5.5 us -> 2.02 us
    pallas_call x1, Pallas kernels: 35.7 us -> 33.6 us  [shards(): pl.pallas_call(functools.partial(kernel, nodes, width), out_shape=pltpu.V...]
    slice x1, local copies, waits for them, and re-layouts: 0.04 us -> 0.81 us  [shards(): rates, weights = (turned[:16], turned[16:])]
where the time goes in v2:
time: 37.6 us; the launch traced here: 37.5 us
  Pallas kernels  33.6 us (89%)
  local copies, waits for them, and re-layouts  2.83 us (8%)
  other arithmetic  1.06 us (3%)
    pallas_call x1, Pallas kernels, shards(): pl.pallas_call(functools.partial(kernel, nodes, width), out_shape=pltpu.V...  33.6 us
    unnamed x1, local copies, waits for them, and re-layouts  2.02 us
    transpose x1, other arithmetic, shards(): turned = jnp.concatenate([decays, residues], 1).T  1.06 us
    slice x1, local copies, waits for them, and re-layouts, shards(): rates, weights = (turned[:16], turned[16:])  0.81 us

profile of v2, /device:TPU:1, one launch (start us, length us, event | category | flops | bytes accessed | tf_op | source)
XLA Modules:
  0.0 37.5 jit_solution(10970858465080744629)
XLA Ops:
  0.0 1.1 %maximum_bitcast_fusion = f32[32,4096]{1,0:T(8,128)S(1)} fusion(f32[4096,16]{0,1:T(8,128)} %param.10, f32[4096,16]{0,1:T(8,128)} %param.9), kind=kLoop, calls=%fused_computation | loop fusion | flops 131072 | bytes 1048576 | tf_op jit(solution)/shard_map/transpose | solution.py:518
  1.1 0.8 %fusion = (f32[16,4096]{1,0:T(8,128)}, f32[16,4096]{1,0:T(8,128)}) fusion(f32[32,4096]{1,0:T(8,128)S(1)} %maximum_bitcast_fusion), kind=kLoop, calls=%fused_computation.1 | loop fusion | bytes 1048576 | tf_op jit(solution)/shard_map/slice | solution.py:519
  1.9 33.6 %hyena.1 = f32[256,4096]{1,0:T(8,128)S(1)} custom-call(bf16[256,12288]{1,0:T(8,128)(2,1)} %proj_hbm.1, f32[7,12288]{1,0:T(8,128)} %taps_hbm.1, f32[16,4096]{1,0:T(8,128)} %get-tuple-element.6.rates_hbm, f32[16,4096]{1,0:T(8,128)} %get-tuple-element.5.weights_hbm, bf16[128,896]{1,0:T(8,128)(2,1)} %constant.6.clone.local_hbm, ...), custom_call_target="tpu_custom_call" | custom-call | tf_op jit(solution)/shard_map/hyena/pallas_call | solution.py:523
  35.5 2.0 %copy.9 = f32[256,4096]{1,0:T(8,128)} copy(f32[256,4096]{1,0:T(8,128)S(1)} %hyena.1) | data formatting | bytes 8388608

commit v3 on v2

--- a/solution.py
+++ b/solution.py
@@ -62,7 +62,7 @@
 
 
 def kernel(
-    nodes, width, proj_hbm, taps_hbm, rates_hbm, weights_hbm, local_hbm, gather_hbm, spread_hbm, queries,
+    nodes, width, proj_hbm, taps_hbm, modes_hbm, local_hbm, gather_hbm, spread_hbm, queries,
     taps, rates, weights, local, gather, spread,
     proj, halo, shifted, gated, conv, coef, send_m, recv_m, send_t, recv_t, send_g, recv_g,
     into, outof, decay, decay_scan, plain_m, scans, carries, plain_g,
@@ -104,7 +104,7 @@
     lax.fori_loop(0, outer, greet_outer, 0)
 
     pairs = (
-        (rates_hbm, rates), (weights_hbm, weights), (taps_hbm, taps),
+        (modes_hbm.at[0:16], rates), (modes_hbm.at[16:32], weights), (taps_hbm, taps),
         (gather_hbm, gather), (local_hbm, local), (spread_hbm, spread),
     )
     small = [pltpu.make_async_copy(a, b, small_sem.at[n]) for n, (a, b) in enumerate(pairs)]
@@ -516,19 +516,18 @@
     outer = lax.axis_size("ctx") // GROUP
     nodes, local, gather, spread = tables()
     turned = jnp.concatenate([decays, residues], 1).T
-    rates, weights = turned[:16], turned[16:]
     hbm = pl.BlockSpec(memory_space=pltpu.HBM)
     dma = pltpu.SemaphoreType.DMA
     steps = width // 512
     return pl.pallas_call(
         functools.partial(kernel, nodes, width),
         out_shape=pltpu.VMEM((rows, width), F32),
-        in_specs=[hbm] * 7,
+        in_specs=[hbm] * 6,
         out_specs=pl.BlockSpec(memory_space=pltpu.VMEM),
         scratch_shapes=[
             pltpu.VMEM(taps.shape, F32),
-            pltpu.VMEM(rates.shape, F32),
-            pltpu.VMEM(weights.shape, F32),
+            pltpu.VMEM((16, width), F32),
+            pltpu.VMEM((16, width), F32),
             pltpu.VMEM(local.shape, BF16),
             pltpu.VMEM(gather.shape, BF16),
             pltpu.VMEM(spread.shape, BF16),
@@ -562,7 +561,7 @@
             collective_id=0, has_side_effects=True, vmem_limit_bytes=60800 * 2**10
         ),
         name="hyena",
-    )(projected, taps, rates, weights, jnp.asarray(local), jnp.asarray(gather), jnp.asarray(spread))
+    )(projected, taps, turned, jnp.asarray(local), jnp.asarray(gather), jnp.asarray(spread))
 
 
 def solution(mesh):

time: 37.6 us -> 37.5 us (level)
  local copies, waits for them, and re-layouts: 2.83 us -> 2.02 us
  other arithmetic: 1.06 us -> 1.86 us
    slice x1 -> x0, local copies, waits for them, and re-layouts: 0.81 us -> none  [shards(): rates, weights = (turned[:16], turned[16:])]
    transpose x1, other arithmetic: 1.06 us -> 1.86 us  [shards(): turned = jnp.concatenate([decays, residues], 1).T]
where the time goes in v3:
time: 37.5 us; the launch traced here: 37.4 us
  Pallas kernels  33.5 us (89%)
  local copies, waits for them, and re-layouts  2.02 us (5%)
  other arithmetic  1.86 us (5%)
    pallas_call x1, Pallas kernels, shards(): pl.pallas_call(functools.partial(kernel, nodes, width), out_shape=pltpu.V...  33.5 us
    unnamed x1, local copies, waits for them, and re-layouts  2.02 us
    transpose x1, other arithmetic, shards(): turned = jnp.concatenate([decays, residues], 1).T  1.86 us

profile of v3, /device:TPU:1, one launch (start us, length us, event | category | flops | bytes accessed | tf_op | source)
XLA Modules:
  0.0 37.4 jit_solution(8046431898548624226)
XLA Ops:
  0.0 1.9 %maximum_bitcast_fusion.modes_hbm = f32[32,4096]{1,0:T(8,128)} fusion(f32[4096,16]{0,1:T(8,128)} %param.10, f32[4096,16]{0,1:T(8,128)} %param.9), kind=kLoop, calls=%fused_computation | loop fusion | flops 131072 | bytes 1048576 | tf_op jit(solution)/shard_map/transpose | solution.py:518
  1.9 33.5 %hyena.1 = f32[256,4096]{1,0:T(8,128)S(1)} custom-call(bf16[256,12288]{1,0:T(8,128)(2,1)} %proj_hbm.1, f32[7,12288]{1,0:T(8,128)} %taps_hbm.1, f32[32,4096]{1,0:T(8,128)} %maximum_bitcast_fusion.modes_hbm, bf16[128,896]{1,0:T(8,128)(2,1)} %constant.6.clone.local_hbm, bf16[32,256]{1,0:T(8,128)(2,1)} %constant.7.clone.gather_hbm, ...), custom_call_target="tpu_custom_call" | custom-call | tf_op jit(solution)/shard_map/hyena/pallas_call | solution.py:522
  35.4 2.0 %copy.9 = f32[256,4096]{1,0:T(8,128)} copy(f32[256,4096]{1,0:T(8,128)S(1)} %hyena.1) | data formatting | bytes 8388608
